TPU v7x, 256 devices: a whole 4x4x8 slice. The times are simulated.
256 devices in a mesh: dp: 32 (over y, z_lo, core), mp: 8 (over z_hi, x).
Axes of the slice: x: 4, y: 4, z: 8 (z_hi: 2, z_lo: 4; z = z_hi * 4 + z_lo), core: 2. Of those that a mesh axis runs over, the one named last changes fastest.
Arguments:
- hidden_acts: bfloat16 [2, 16384, 12288], P(None, 'dp', 'mp'), may hold values from -6 to 6
- out_grads: bfloat16 [2, 16384, 3072], P(None, 'dp', 'mp'), may hold values from -6 to 6
- token_picks: int32 [32, 512], P('dp'), may hold values from 0 to 511, each once within a row
- weight_grads: bfloat16 [2, 12288, 3072], P(None, 'dp', 'mp'), may hold values from -6 to 6
Outputs:
- preconditioned: bfloat16 [2, 12288, 3072], P(None, 'dp', 'mp')
Inputs may be any that keep to these rules, and one draw needn't show every extreme that they name: `token_picks`: each row is an ordering of 0 to 511; its first 256 entries name the sampled tokens.
All inputs are finite; a program needn't handle non-finite values. Where the computation divides by a largest or mean magnitude, that divisor is 1e-20 or more.
Results may differ from a plain program's by a relative error of at most 0.0066.
Values may be sent and summed in bfloat16 or wider, within the bound.
A program may use at most 128 MiB of HBM per device.

v0:
```python
import jax
import jax.numpy as jnp
from jax import lax
from jax.sharding import PartitionSpec as P

BLK = 384
ITERS = 5
SAMPLE = 256


damping = 0.1
highest = lax.Precision.HIGHEST


def from_root(block, axis, source):
    block = jnp.where(lax.axis_index(axis) == source, block, jnp.zeros_like(block))
    return lax.psum(block, axis)


def batched(first, second):
    return jnp.einsum(
        "kab,kbc->kac", first, second, precision=highest, preferred_element_type=jnp.float32
    )


def newton_start(factor):
    row_bound = jnp.max(jnp.sum(jnp.abs(factor), axis=-1), axis=-1)
    identity = jnp.eye(factor.shape[-1], dtype=jnp.float32)
    return identity[None] / row_bound[:, None, None]


def newton_full(factor):
    approx = newton_start(factor)
    for sweep in range(ITERS):
        approx = 2.0 * approx - batched(approx, batched(factor, approx))
    return approx


def invert_owned(factor, devices, position):
    tile_count, tile_size = (factor.shape[0], factor.shape[-1])
    slot_count = -(-tile_count // devices)
    spare = slot_count * devices - tile_count
    filler = jnp.broadcast_to(
        damping * jnp.eye(tile_size, dtype=jnp.float32), (spare, tile_size, tile_size)
    )
    padded = jnp.concatenate([factor, filler], axis=0).reshape(
        slot_count, devices, tile_size, tile_size
    )
    owned = lax.dynamic_index_in_dim(padded, position, 1, keepdims=False)
    inverse = newton_full(owned).astype(jnp.bfloat16)
    pieces = [
        from_root(inverse[tile_index // devices], "dp", tile_index % devices)
        for tile_index in range(tile_count)
    ]
    return jnp.stack(pieces)


def invert_grad_tiles(factor, devices, position):
    return invert_owned(factor, devices, position)


def tile_gram(chosen):
    tile_stack = chosen.reshape(chosen.shape[0], chosen.shape[1], -1, BLK)
    return jnp.einsum("lsta,lstb->ltab", tile_stack, tile_stack, preferred_element_type=jnp.float32)


def shards(hidden_acts, out_grads, token_picks, weight_grads):
    layers = hidden_acts.shape[0]
    identity = jnp.eye(BLK, dtype=jnp.float32)
    dp_count = lax.axis_size("dp")
    dp_pos = lax.axis_index("dp")
    picks = token_picks[0, :SAMPLE]
    chosen_grads = jnp.take(out_grads, picks, axis=1)
    chosen_hidden = jnp.take(hidden_acts, picks, axis=1)
    g_total = lax.psum(tile_gram(chosen_grads), "dp")
    g_factor = g_total / (SAMPLE * dp_count) + damping * identity
    a_gram = tile_gram(chosen_hidden)
    group_tiles = a_gram.shape[1]
    own_tiles = weight_grads.shape[1] // BLK
    offset = dp_pos * own_tiles % group_tiles
    root = dp_pos * own_tiles // group_tiles
    a_total = lax.psum(a_gram, "dp")
    needed = lax.dynamic_slice_in_dim(a_total, offset, own_tiles, 1)
    a_factor = needed / (SAMPLE * dp_count) + damping * identity
    a_local = (
        newton_full(a_factor.reshape(-1, BLK, BLK))
        .astype(jnp.bfloat16)
        .reshape(layers, own_tiles, BLK, BLK)
    )
    a_inverse = from_root(a_local, "mp", root)
    g_tiles = g_factor.shape[1]
    g_inverse = invert_grad_tiles(g_factor.reshape(-1, BLK, BLK), dp_count, dp_pos).reshape(
        layers, g_tiles, BLK, BLK
    )
    grad_tiles = weight_grads.reshape(layers, own_tiles, BLK, g_tiles, BLK)
    left_product = jnp.einsum(
        "lrab,lrbcd->lracd", a_inverse, grad_tiles, preferred_element_type=jnp.float32
    ).astype(jnp.bfloat16)
    result = jnp.einsum(
        "lracd,lcde->lrace", left_product, g_inverse, preferred_element_type=jnp.float32
    ).astype(jnp.bfloat16)
    return result.reshape(layers, own_tiles * BLK, g_tiles * BLK)


def solution(mesh):
    placed = (P(None, "dp", "mp"), P(None, "dp", "mp"), P("dp", None), P(None, "dp", "mp"))
    return jax.shard_map(
        shards, mesh=mesh, in_specs=placed, out_specs=P(None, "dp", "mp"), check_vma=False
    )
```

profile of v0, /device:TPU:2, one launch (start us, length us, event | category | flops | bytes accessed | tf_op | source)
XLA Modules:
  0.0 745.4 jit_solution(11625958927035750990)
XLA Ops:
  6.5 0.8 compare_select_fusion
  7.4 0.8 slice.3
  8.2 3.8 gather_fusion
  12.1 6.5 gather_fusion.1
  18.6 2.6 copy.28
  21.2 1.6 convolution_bitcast_fusion
  22.8 3.2 fusion
  25.9 0.0 all-reduce.8.cloned.1.call-update
  26.0 0.2 all-reduce.6.cloned.1.call-start
  26.2 0.9 fusion.40
  27.1 0.8 fusion.39
  27.9 302.4 %all-reduce.8.cloned.1.call-done = (f32[2,4,384,384]{3,2,0,1:T(8,128)}, f32[2,1,384,384]{3,2,0,1:T(8,128)}) async-done(((f32[2,4,384,384]{3,2,0,1:T(8,128)}, f32[2,1,384,384]{3,2,0,1:T(8,128)}), (f32[2,4,384,384]{3,2,0,1:T(8,128)}, f32[2,1,384,384]{3,2,0,1:T(8,128)})) %all-reduce.8.cloned.1.call-update) | async-done | bytes 5898256 | tf_op jit(solution)/shard_map/psum | solution.py:82
  330.3 2.7 fusion.16
  333.0 0.1 reduce_max.19
  333.1 4.0 fusion.14
  337.2 2.5 convolution_subtract_fusion.4
  339.7 2.4 fusion.12
  342.1 2.4 convolution_subtract_fusion.3
  344.6 2.9 fusion.10
  347.4 2.4 convolution_subtract_fusion.2
  349.9 2.4 fusion.8
  352.3 2.4 convolution_subtract_fusion.1
  354.8 2.4 fusion.6
  357.2 3.5 fusion.4
  360.7 0.0 all-reduce.6.cloned.1.call-update
  360.7 0.0 all-reduce.10.cloned.1.call-start
  360.8 0.0 copy-start.3
  360.8 1.6 add_bitcast_fusion
  362.4 0.0 copy-done.3
  362.4 8.0 %broadcast_in_dim.34 = f32[30,384,384]{2,1,0:T(8,128)} broadcast(f32[384,384]{1,0:T(8,128)S(1)} %copy-done.3), dimensions={1,2} | broadcast | bytes 18284544 | tf_op jit(solution)/shard_map/broadcast_in_dim | solution.py:43
  370.4 0.9 abs_reduce_fusion
  371.4 0.6 reduce_max.18
  372.7 0.0 copy-start.2
  372.7 2.2 fusion.20
  374.9 1.2 convolution_subtract_fusion.9
  376.2 1.3 fusion.32
  377.4 1.3 convolution_subtract_fusion.8
  378.7 1.3 fusion.30
  380.0 1.3 convolution_subtract_fusion.7
  381.2 1.3 fusion.28
  382.5 1.3 convolution_subtract_fusion.6
  383.8 1.5 fusion.26
  385.3 2.1 select_bitcast_fusion.1
  387.3 0.0 all-reduce.10.cloned.1.call-update
  387.4 74.6 %all-reduce.6.cloned.1.call-done = bf16[2,384,384]{2,1,0:T(8,128)(2,1)} async-done(((bf16[2,384,384]{2,1,0:T(8,128)(2,1)}), bf16[2,384,384]{2,1,0:T(8,128)(2,1)}) %all-reduce.6.cloned.1.call-update) | async-done | bytes 589840 | tf_op jit(solution)/shard_map/psum | solution.py:17
  462.0 271.4 %all-reduce.10.cloned.1.call-done = (bf16[1,384,384]{2,1,0:T(8,128)(2,1)}, bf16[1,384,384]{2,1,0:T(8,128)(2,1)}) async-done(((bf16[1,384,384]{2,1,0:T(8,128)(2,1)}, bf16[1,384,384]{2,1,0:T(8,128)(2,1)}), (bf16[1,384,384]{2,1,0:T(8,128)(2,1)}, bf16[1,384,384]{2,1,0:T(8,128)(2,1)})) %all-reduce.10.cloned.1.call-update) | async-done | bytes 589840 | tf_op jit(solution)/shard_map/psum | solution.py:17
  733.4 3.1 fusion.3
  736.5 2.1 copy.22
  (12 shorter events, 0.0 us)
Async XLA Ops:
  6.5 5.5 copy-start
  6.5 323.8 %all-reduce.8.cloned.1.call-start = ((), (), s32[]{:S(2)}) async-start(), calls=%async_computation.1 | async-start | bytes 11796480 | tf_op jit(solution)/shard_map/psum | solution.py:82
  21.2 1.6 copy-start.4
  26.0 436.0 %all-reduce.6.cloned.1.call-start = ((), (), s32[]{:S(2)}) async-start(), calls=%async_computation | async-start | bytes 1179648 | tf_op jit(solution)/shard_map/psum | solution.py:17
  333.1 4.0 copy-start.5
  337.2 2.5 copy-start.1
  360.7 372.7 %all-reduce.10.cloned.1.call-start = ((), (), s32[]{:S(2)}) async-start(), calls=%async_computation.2 | async-start | bytes 1179648 | tf_op jit(solution)/shard_map/psum | solution.py:17
  360.8 1.6 copy-start.3
  372.7 3.5 copy-start.2
Sparse Core Ops, SparseCore 0:
  26.1 304.2 all-reduce.7
  360.8 101.0 all-reduce.5
  464.7 268.6 all-reduce.9
where the time goes:
time: 752 us; the launch traced here: 745 us
  waiting for transfers between devices  648 us (86%)
  matrix products  49.9 us (7%)
  local copies, waits for them, and re-layouts  24 us (3%)
  between operations  14.3 us (2%)
  other arithmetic  8.49 us (1%)
    psum x2, waiting for transfers between devices, from_root(): return lax.psum(block, axis)  346 us
    psum x1, waiting for transfers between devices, shards(): a_total = lax.psum(a_gram, 'dp')  302 us
    dot_general x20, matrix products, batched(): jnp.einsum('kab,kbc->kac', first, second, precision=highest, preferred_el...  42.1 us
  transfers between devices with their start and end apart: 3, of which 3 were waited for; matrix products, arithmetic and copies ran while one was open for 4% of the time, Pallas kernels for 0%

commit v1 on v0

v1 whole, which is shorter than its diff:
```python
import jax
import jax.numpy as jnp
from jax import lax
from jax.experimental import pallas as pl
from jax.experimental.pallas import tpu as pltpu
from jax.sharding import PartitionSpec as P

BLK = 384
SAMPLE = 256
POOL = 512
ROWS = 768
PART = 192
DAMPING = 0.1
MESH = pl.DeviceIdType.MESH
F32 = jnp.float32
BF16 = jnp.bfloat16
GROUPS = ((0, 2), (2, 2), (4, 1))
BLOCKS = ((0, 0), (0, 1), (0, 2), (1, 1), (1, 2), (2, 2))


def kernel(
    hid_hbm, grd_hbm, picks, w_hbm, out,
    hid, grd, wv, mask, abuf, arec, own, s1, brec, ysum, cs, crec, grec, dtot, gtot, ft, lhs, rhs, acc, ginv, left,
    load_sem, a_s, a_r, b_s, b_r, c_s, c_r, g_s, g_r, d_s, d_r, e_s, e_r, h_s, h_r, i_s, i_r,
):
    i, m = lax.axis_index("dp"), lax.axis_index("mp")
    c, z, y = lax.rem(i, 2), lax.rem(i // 2, 4), i // 8
    zh, x = m // 4, lax.rem(m, 4)
    active = z // 2 == lax.rem(x, 2)
    x_src = lax.rem(y, 2) * 2 + z // 2

    def dev(y=y, z=z, c=c, zh=zh, x=x):
        return ((y * 4 + z) * 2 + c, zh * 4 + x)

    def turn(v, by):
        return lax.rem(v + by, 4)

    def send(src, dst, ss, rs, to):
        return pltpu.make_async_remote_copy(
            src_ref=src, dst_ref=dst, send_sem=ss, recv_sem=rs, device_id=to, device_id_type=MESH
        )

    def part(q):
        return pl.ds(pl.multiple_of(q * PART, PART), PART)

    barrier = pltpu.get_barrier_semaphore()

    def greet(to):
        pl.semaphore_signal(barrier, inc=1, device_id=to, device_id_type=MESH)

    greet(dev(c=1 - c))
    greet(dev(zh=1 - zh))
    for by in (1, 2, 3):
        greet(dev(y=turn(y, by)))
        greet(dev(z=turn(z, by)))
    for cc in (0, 1):
        for by in range(4):
            if by:
                greet(dev(x=x_src, y=turn(y, by), c=cc))
            else:
                @pl.when((x_src != x) | (c != cc))
                def _():
                    greet(dev(x=x_src, c=cc))

    other = 1 - c
    loads = []
    for n, (src, dst) in enumerate((
        (hid_hbm.at[other], hid.at[other]), (grd_hbm.at[other], grd.at[other]),
        (hid_hbm.at[c], hid.at[c]), (grd_hbm.at[c], grd.at[c]), (w_hbm, wv),
    )):
        loads.append(pltpu.make_async_copy(src, dst, load_sem.at[n]))
        loads[-1].start()

    token = lax.broadcasted_iota(jnp.int32, (POOL, SAMPLE), 0)
    hit = jnp.where(token == picks[:, :SAMPLE], 1.0, 0.0)
    mask[...] = jnp.broadcast_to(jnp.max(hit, axis=1, keepdims=True), (POOL, BLK)).astype(BF16)

    def gram(tile, dst):
        masked = tile * mask[...]
        row = 0
        for r in range(3):
            g = lax.dot_general(
                masked[:, r * 128 : (r + 1) * 128], tile[:, r * 128 :], (((0,), (0,)), ((), ())),
                preferred_element_type=F32,
            )
            for k in range(3 - r):
                dst[row : row + 128, :] = g[:, k * 128 : (k + 1) * 128].astype(dst.dtype)
                row += 128

    def grams(layer, first, count, dst):
        if count == 1:
            gram(grd[layer], dst.at[first])
        else:
            def body(t, _):
                gram(hid[layer, :, pl.ds(pl.multiple_of(t * BLK, 128), BLK)], dst.at[t])
                return 0

            lax.fori_loop(first, first + count, body, 0)

    started = []
    for g, (first, count) in enumerate(GROUPS):
        if g != 1:
            loads[0 if g == 0 else 1].wait()
        grams(other, first, count, abuf)
        if g == 0:
            pl.semaphore_wait(barrier, 8 + jnp.where(active, jnp.where(lax.rem(y, 2) == x // 2, 15, 16), 0))
        span = pl.ds(first, count)
        copy = send(abuf.at[span], arec.at[span], a_s.at[g], a_r.at[g], dev(c=other))
        copy.start()
        started.append(copy)
    loads[2].wait()
    loads[3].wait()
    for first, count in GROUPS:
        grams(c, first, count, own)

    from_sibling = list(started)
    from_y = {}
    for g, (first, count) in enumerate(GROUPS):
        from_sibling[g].wait_recv()
        for t in range(first, first + count):
            total = own[t] + arec[t].astype(F32)
            own[t] = total
            s1[t] = total.astype(BF16)
        span = pl.ds(first, count)
        for by in (1, 2, 3):
            to = turn(y, by)
            copy = send(
                s1.at[span, part(to)], brec.at[by - 1, span], b_s.at[g, by - 1], b_r.at[g, by - 1], dev(y=to)
            )
            copy.start()
            started.append(copy)
            from_y[g, by] = copy

    from_z = {}
    for g, (first, count) in enumerate(GROUPS):
        for by in (1, 2, 3):
            from_y[g, by].wait_recv()
        for t in range(first, first + count):
            total = own[t, part(y)]
            for by in (1, 2, 3):
                total += brec[by - 1, t].astype(F32)
            ysum[t] = total
            cs[t] = total.astype(BF16)
        if g < 2:
            goal = 2 * lax.rem(x, 2) + g

            @pl.when(z != goal)
            def _():
                slot = lax.rem(z - goal + 4, 4) - 1
                send(cs.at[pl.ds(first, 2)], crec.at[slot], c_s.at[g], c_r.at[slot], dev(z=goal)).start()
        else:
            for by in (1, 2, 3):
                copy = send(cs.at[4], grec.at[by - 1], g_s.at[by - 1], g_r.at[by - 1], dev(z=turn(z, by)))
                copy.start()
                started.append(copy)
                from_z[by] = copy

    def spread(plane):
        y_goal = plane * 2 + x // 2
        for e in (0, 1):
            for by in range(4):
                copy = send(
                    dtot.at[plane, e], ft.at[c, part(y)], e_s.at[plane, e, by], e_r.at[c, y],
                    dev(y=y_goal, c=e, x=turn(x, by)),
                )
                if by:
                    copy.start()
                else:
                    here = (y_goal == y) & (c == e)

                    @pl.when(here)
                    def _():
                        ft[c, part(y)] = dtot[plane, e]

                    @pl.when(jnp.logical_not(here))
                    def _():
                        copy.start()

    cross = send(dtot.at[zh], dtot.at[zh], d_s, d_r, dev(zh=1 - zh))

    @pl.when(active)
    def _():
        for by in (1, 2, 3):
            send(cs.at[pl.ds(0, 2)], crec.at[by - 1], c_s.at[0], c_r.at[by - 1], dev(c=other)).wait_recv()
        for e in (0, 1):
            total = ysum[2 * lax.rem(z, 2) + e]
            for by in (1, 2, 3):
                total += crec[by - 1, e].astype(F32)
            dtot[zh, e] = total.astype(BF16)
        cross.start()
        spread(zh)

    for by in (1, 2, 3):
        from_z[by].wait_recv()
    total = ysum[4]
    for by in (1, 2, 3):
        total += grec[by - 1].astype(F32)
    gtot[...] = total.astype(BF16)
    ft[2, part(y)] = gtot[...]
    for by in (1, 2, 3):
        copy = send(gtot, ft.at[2, part(y)], h_s.at[by - 1], h_r.at[by - 1], dev(y=turn(y, by)))
        copy.start()
        started.append(copy)

    @pl.when(active)
    def _():
        send(dtot.at[zh], dtot.at[1 - zh], d_s, d_r, dev(zh=1 - zh)).wait_recv()
        spread(1 - zh)

    def inverse(slot):
        block = {rc: ft[slot, n * 128 : (n + 1) * 128].astype(F32) for n, rc in enumerate(BLOCKS)}
        for r in range(3):
            for k in range(3):
                tile = block[r, k] if r <= k else block[k, r].T
                acc[r * 128 : (r + 1) * 128, k * 128 : (k + 1) * 128] = tile
        eye = jnp.where(
            lax.broadcasted_iota(jnp.int32, (BLK, BLK), 0) == lax.broadcasted_iota(jnp.int32, (BLK, BLK), 1), 1.0, 0.0
        )
        factor = acc[...] * (1.0 / 8192.0) + DAMPING * eye
        bound = jnp.max(jnp.sum(jnp.abs(factor), axis=1, keepdims=True), axis=0, keepdims=True)
        step = 1.0 / bound

        def put(value, column):
            high = value.astype(BF16)
            low = (value - high.astype(F32)).astype(BF16)
            span = slice(column * BLK, (column + 1) * BLK)
            rhs[0:BLK, span] = high
            rhs[BLK : 2 * BLK, span] = low
            rhs[2 * BLK :, span] = high
            if column == 0:
                lhs[:, 0:BLK] = high
                lhs[:, BLK : 2 * BLK] = high
                lhs[:, 2 * BLK :] = low

        residue = eye - factor * step
        acc[...] = eye + residue
        put(residue, 0)
        put(acc[...], 1)
        put(jnp.dot(lhs[...], rhs[:, :BLK], preferred_element_type=F32), 0)
        for _ in range(3):
            both = jnp.dot(lhs[...], rhs[...], preferred_element_type=F32)
            acc[...] += both[:, BLK:]
            put(both[:, :BLK], 0)
            put(acc[...], 1)
        acc[...] += jnp.dot(lhs[...], rhs[:, BLK:], preferred_element_type=F32)
        return (acc[...] * step).astype(BF16)

    for by in (1, 2, 3):
        send(gtot, ft.at[2, part(y)], h_s.at[by - 1], h_r.at[by - 1], dev(y=turn(y, by))).wait_recv()
    ginv[c] = inverse(2)
    swap = send(ginv.at[c], ginv.at[c], i_s, i_r, dev(c=other))
    swap.start()
    loads[4].wait()

    def layer_step(layer, _):
        for yy in range(4):
            mine = (x == x_src) & (c == layer) & (y == yy)

            @pl.when(jnp.logical_not(mine))
            def _():
                send(
                    dtot.at[0, 0], ft.at[layer, part(yy)], e_s.at[0, 0, 0], e_r.at[layer, yy], dev(c=other)
                ).wait_recv()
        left[layer] = jnp.dot(inverse(layer), wv[layer], preferred_element_type=F32).astype(BF16)
        return 0

    lax.fori_loop(0, 2, layer_step, 0)
    swap.wait()
    for layer in (0, 1):
        out[layer] = jnp.dot(left[layer], ginv[layer], preferred_element_type=F32).astype(BF16)

    for copy in started:
        copy.wait_send()
    for g in (0, 1):
        @pl.when(z != 2 * lax.rem(x, 2) + g)
        def _():
            send(cs.at[pl.ds(0, 2)], crec.at[0], c_s.at[g], c_r.at[0], dev(c=other)).wait_send()

    @pl.when(active)
    def _():
        cross.wait_send()
        for plane in (0, 1):
            for e in (0, 1):
                for by in range(4):
                    copy = send(dtot.at[0, 0], ft.at[0, part(0)], e_s.at[plane, e, by], e_r.at[0, 0], dev(c=other))
                    if by:
                        copy.wait_send()
                    else:
                        @pl.when((plane * 2 + x // 2 != y) | (c != e))
                        def _():
                            copy.wait_send()


def shards(hidden_acts, out_grads, token_picks, weight_grads):
    dma = pltpu.SemaphoreType.DMA
    vmem = pltpu.VMEM
    return pl.pallas_call(
        kernel,
        out_shape=jax.ShapeDtypeStruct(weight_grads.shape, BF16),
        in_specs=[
            pl.BlockSpec(memory_space=pl.ANY),
            pl.BlockSpec(memory_space=pl.ANY),
            pl.BlockSpec(memory_space=vmem),
            pl.BlockSpec(memory_space=pl.ANY),
        ],
        out_specs=pl.BlockSpec(memory_space=vmem),
        scratch_shapes=[
            vmem(hidden_acts.shape, BF16), vmem(out_grads.shape, BF16), vmem(weight_grads.shape, BF16),
            vmem((POOL, BLK), BF16),
            vmem((5, ROWS, 128), BF16), vmem((5, ROWS, 128), BF16), vmem((5, ROWS, 128), F32), vmem((5, ROWS, 128), BF16),
            vmem((3, 5, PART, 128), BF16), vmem((5, PART, 128), F32), vmem((5, PART, 128), BF16),
            vmem((3, 2, PART, 128), BF16), vmem((3, PART, 128), BF16), vmem((2, 2, PART, 128), BF16),
            vmem((PART, 128), BF16), vmem((3, ROWS, 128), BF16),
            vmem((BLK, 3 * BLK), BF16), vmem((3 * BLK, 2 * BLK), BF16), vmem((BLK, BLK), F32),
            vmem((2, BLK, BLK), BF16), vmem((2, BLK, BLK), BF16),
            dma((5,)), dma((3,)), dma((3,)), dma((3, 3)), dma((3, 3)), dma((2,)), dma((3,)), dma((3,)), dma((3,)),
            dma, dma, dma((2, 2, 4)), dma((2, 4)), dma((3,)), dma((3,)), dma, dma,
        ],
        compiler_params=pltpu.CompilerParams(
            collective_id=0, has_side_effects=True, vmem_limit_bytes=48 * 2**20
        ),
    )(hidden_acts, out_grads, token_picks, weight_grads)


def solution(mesh):
    placed = (P(None, "dp", "mp"), P(None, "dp", "mp"), P("dp", None), P(None, "dp", "mp"))
    return jax.shard_map(shards, mesh=mesh, in_specs=placed, out_specs=P(None, "dp", "mp"), check_vma=False)
```

time: 752 us -> 60 us (0.08)
  the two profiles are of different devices: /device:TPU:2 before, /device:TPU:28 now
where the time goes in v1:
time: 60 us; the launch traced here: 59.8 us
  Pallas kernels  54.2 us (90%)
  local copies, waits for them, and re-layouts  5.58 us (9%)
    pallas_call x1, Pallas kernels, shards(): pl.pallas_call(kernel, out_shape=jax.ShapeDtypeStruct(weight_grads.shape,...  54.2 us
    unnamed x9, local copies, waits for them, and re-layouts  5.58 us

profile of v1, /device:TPU:28, one launch (start us, length us, event | category | flops | bytes accessed | tf_op | source)
XLA Modules:
  0.0 59.8 jit_solution(13532570713654059415)
XLA Ops:
  0.0 0.0 copy-start
  0.0 1.9 %copy-done = bf16[2,512,1536]{2,1,0:T(8,128)(2,1)S(1)} copy-done((bf16[2,512,1536]{2,1,0:T(8,128)(2,1)S(1)}, bf16[2,512,1536]{2,1,0:T(8,128)(2,1)}, u32[]{:S(2)}) %copy-start) | copy-done | bytes 3145752
  1.9 0.0 copy-start.1
  1.9 1.1 %copy-done.1 = bf16[2,512,384]{2,1,0:T(8,128)(2,1)S(1)} copy-done((bf16[2,512,384]{2,1,0:T(8,128)(2,1)S(1)}, bf16[2,512,384]{2,1,0:T(8,128)(2,1)}, u32[]{:S(2)}) %copy-start.1) | copy-done | bytes 786456
  3.0 0.0 copy-start.2
  3.0 1.1 %copy-done.2 = bf16[2,384,384]{2,1,0:T(8,128)(2,1)S(1)} copy-done((bf16[2,384,384]{2,1,0:T(8,128)(2,1)S(1)}, bf16[2,384,384]{2,1,0:T(8,128)(2,1)}, u32[]{:S(2)}) %copy-start.2) | copy-done | bytes 589848
  4.1 0.0 copy-start.3
  4.1 0.7 %copy-done.3 = s32[1,512]{1,0:T(1,128)S(1)} copy-done((s32[1,512]{1,0:T(1,128)S(1)}, s32[1,512]{1,0:T(1,128)}, u32[]{:S(2)}) %copy-start.3) | copy-done | bytes 2072
  4.8 54.2 %shard_map.46 = bf16[2,384,384]{2,1,0:T(8,128)(2,1)S(1)} custom-call(bf16[2,512,1536]{2,1,0:T(8,128)(2,1)S(1)} %copy-done, bf16[2,512,384]{2,1,0:T(8,128)(2,1)S(1)} %copy-done.1, s32[1,512]{1,0:T(1,128)S(1)} %copy-done.3, bf16[2,384,384]{2,1,0:T(8,128)(2,1)S(1)} %copy-done.2), custom_call_target="tpu_custom_call" | custom-call | tf_op jit(solution)/shard_map/pallas_call | solution.py:297
  59.0 0.8 %copy.6 = bf16[2,384,384]{2,1,0:T(8,128)(2,1)} copy(bf16[2,384,384]{2,1,0:T(8,128)(2,1)S(1)} %shard_map.46) | data formatting | bytes 1179648
Async XLA Ops:
  0.0 1.9 %copy-start = (bf16[2,512,1536]{2,1,0:T(8,128)(2,1)S(1)}, bf16[2,512,1536]{2,1,0:T(8,128)(2,1)}, u32[]{:S(2)}) copy-start(bf16[2,512,1536]{2,1,0:T(8,128)(2,1)} %hid_hbm.1) | copy-start | bytes 9437188
  1.9 1.1 %copy-start.1 = (bf16[2,512,384]{2,1,0:T(8,128)(2,1)S(1)}, bf16[2,512,384]{2,1,0:T(8,128)(2,1)}, u32[]{:S(2)}) copy-start(bf16[2,512,384]{2,1,0:T(8,128)(2,1)} %grd_hbm.1) | copy-start | bytes 2359300
  3.0 1.1 %copy-start.2 = (bf16[2,384,384]{2,1,0:T(8,128)(2,1)S(1)}, bf16[2,384,384]{2,1,0:T(8,128)(2,1)}, u32[]{:S(2)}) copy-start(bf16[2,384,384]{2,1,0:T(8,128)(2,1)} %w_hbm.1) | copy-start | bytes 1769476
  4.1 0.7 %copy-start.3 = (s32[1,512]{1,0:T(1,128)S(1)}, s32[1,512]{1,0:T(1,128)}, u32[]{:S(2)}) copy-start(s32[1,512]{1,0:T(1,128)} %picks.1) | copy-start | bytes 6148

commit v2 on v1

v2 whole, which is shorter than its diff:
```python
import jax
import jax.numpy as jnp
from jax import lax
from jax.experimental import pallas as pl
from jax.experimental.pallas import tpu as pltpu
from jax.sharding import PartitionSpec as P

BLK = 384
SAMPLE = 256
POOL = 512
ROWS = 768
PART = 192
DAMPING = 0.1
MESH = pl.DeviceIdType.MESH
F32 = jnp.float32
BF16 = jnp.bfloat16
ORDER = (0, 2, 4, 1, 3)
BLOCKS = ((0, 0), (0, 1), (0, 2), (1, 1), (1, 2), (2, 2))


def kernel(
    hid_hbm, grd_hbm, picks, w_hbm, out,
    hid, grd, wv, mask, abuf, arec, own, s1, brec, ysum, cs, crec, grec, dtot, gtot, ft, lhs, rhs, acc, ginv, left,
    load_sem, a_s, a_r, b_s, b_r, c_s, c_r, g_s, g_r, d_s, d_r, e_s, e_r, h_s, h_r, i_s, i_r,
):
    i, m = lax.axis_index("dp"), lax.axis_index("mp")
    c, z, y = lax.rem(i, 2), lax.rem(i // 2, 4), i // 8
    zh, x = m // 4, lax.rem(m, 4)
    active = z // 2 == lax.rem(x, 2)
    x_src = lax.rem(y, 2) * 2 + z // 2

    def dev(y=y, z=z, c=c, zh=zh, x=x):
        return ((y * 4 + z) * 2 + c, zh * 4 + x)

    def turn(v, by):
        return lax.rem(v + by, 4)

    def send(src, dst, ss, rs, to):
        return pltpu.make_async_remote_copy(
            src_ref=src, dst_ref=dst, send_sem=ss, recv_sem=rs, device_id=to, device_id_type=MESH
        )

    def part(q):
        return pl.ds(pl.multiple_of(q * PART, PART), PART)

    barrier = pltpu.get_barrier_semaphore()

    def greet(to):
        pl.semaphore_signal(barrier, inc=1, device_id=to, device_id_type=MESH)

    greet(dev(c=1 - c))
    greet(dev(zh=1 - zh))
    for by in (1, 2, 3):
        greet(dev(y=turn(y, by)))
        greet(dev(z=turn(z, by)))
    for cc in (0, 1):
        for by in range(4):
            if by:
                greet(dev(x=x_src, y=turn(y, by), c=cc))
            else:
                @pl.when((x_src != x) | (c != cc))
                def _():
                    greet(dev(x=x_src, c=cc))

    other = 1 - c
    loads = {}
    for n, (own_layer, t) in enumerate([(own_layer, t) for own_layer in (0, 1) for t in ORDER]):
        layer = c if own_layer else other
        if t == 4:
            copy = pltpu.make_async_copy(grd_hbm.at[layer], grd.at[layer], load_sem.at[n])
        else:
            span = pl.ds(t * BLK, BLK)
            copy = pltpu.make_async_copy(hid_hbm.at[layer, :, span], hid.at[layer, :, span], load_sem.at[n])
        copy.start()
        loads[own_layer, t] = copy
    load_w = pltpu.make_async_copy(w_hbm, wv, load_sem.at[10])
    load_w.start()

    token = lax.broadcasted_iota(jnp.int32, (POOL, SAMPLE), 0)
    hit = jnp.where(token == picks[:, :SAMPLE], 1.0, 0.0)
    mask[...] = jnp.broadcast_to(jnp.max(hit, axis=1, keepdims=True), (POOL, BLK)).astype(BF16)

    def gram(tile, dst):
        masked = tile * mask[...]
        row = 0
        for r in range(3):
            g = lax.dot_general(
                masked[:, r * 128 : (r + 1) * 128], tile[:, r * 128 :], (((0,), (0,)), ((), ())),
                preferred_element_type=F32,
            )
            for k in range(3 - r):
                dst[row : row + 128, :] = g[:, k * 128 : (k + 1) * 128].astype(dst.dtype)
                row += 128

    def gram_of(own_layer, t, dst):
        loads[own_layer, t].wait()
        layer = c if own_layer else other
        gram(grd[layer] if t == 4 else hid[layer, :, t * BLK : (t + 1) * BLK], dst.at[t])

    started, from_sibling, from_y, from_z = [], {}, {}, {}
    for n, t in enumerate(ORDER):
        gram_of(0, t, abuf)
        if n == 0:
            pl.semaphore_wait(barrier, 8 + jnp.where(active, jnp.where(lax.rem(y, 2) == x // 2, 15, 16), 0))
        copy = send(abuf.at[t], arec.at[t], a_s.at[t], a_r.at[t], dev(c=other))
        copy.start()
        started.append(copy)
        from_sibling[t] = copy
    for t in ORDER:
        gram_of(1, t, own)

    for t in ORDER:
        from_sibling[t].wait_recv()
        total = own[t] + arec[t].astype(F32)
        own[t] = total
        s1[t] = total.astype(BF16)
        for by in (2, 1, 3):
            to = turn(y, by)
            copy = send(s1.at[t, part(to)], brec.at[by - 1, t], b_s.at[t, by - 1], b_r.at[t, by - 1], dev(y=to))
            copy.start()
            started.append(copy)
            from_y[t, by] = copy

    def sum_y(t):
        for by in (1, 2, 3):
            from_y[t, by].wait_recv()
        total = own[t, part(y)]
        for by in (1, 2, 3):
            total += brec[by - 1, t].astype(F32)
        ysum[t] = total
        cs[t] = total.astype(BF16)

    def to_users(t):
        sum_y(t)
        goal = 2 * lax.rem(x, 2) + t // 2

        @pl.when(z != goal)
        def _():
            slot = lax.rem(z - goal + 4, 4) - 1
            send(cs.at[t], crec.at[slot, t % 2], c_s.at[t], c_r.at[slot, t % 2], dev(z=goal)).start()

    def spread(plane, e):
        y_goal = plane * 2 + x // 2
        for by in (2, 1, 3, 0):
            copy = send(
                dtot.at[plane, e], ft.at[c, part(y)], e_s.at[plane, e, by], e_r.at[c, y],
                dev(y=y_goal, c=e, x=turn(x, by)),
            )
            if by:
                copy.start()
            else:
                here = (y_goal == y) & (c == e)

                @pl.when(here)
                def _():
                    ft[c, part(y)] = dtot[plane, e]

                @pl.when(jnp.logical_not(here))
                def _():
                    copy.start()

    def cross(e):
        return send(dtot.at[zh, e], dtot.at[zh, e], d_s.at[e], d_r.at[e], dev(zh=1 - zh))

    def own_plane(e):
        @pl.when(active)
        def _():
            for by in (1, 2, 3):
                send(cs.at[0], crec.at[by - 1, e], c_s.at[0], c_r.at[by - 1, e], dev(c=other)).wait_recv()
            total = ysum[2 * lax.rem(z, 2) + e]
            for by in (1, 2, 3):
                total += crec[by - 1, e].astype(F32)
            dtot[zh, e] = total.astype(BF16)
            cross(e).start()
            spread(zh, e)

    def other_plane(e):
        @pl.when(active)
        def _():
            send(dtot.at[zh, e], dtot.at[1 - zh, e], d_s.at[e], d_r.at[e], dev(zh=1 - zh)).wait_recv()
            spread(1 - zh, e)

    to_users(0)
    to_users(2)
    sum_y(4)
    for by in (1, 2, 3):
        copy = send(cs.at[4], grec.at[by - 1], g_s.at[by - 1], g_r.at[by - 1], dev(z=turn(z, by)))
        copy.start()
        started.append(copy)
        from_z[by] = copy
    own_plane(0)
    to_users(1)
    to_users(3)
    other_plane(0)
    for by in (1, 2, 3):
        from_z[by].wait_recv()
    total = ysum[4]
    for by in (1, 2, 3):
        total += grec[by - 1].astype(F32)
    gtot[...] = total.astype(BF16)
    ft[2, part(y)] = gtot[...]
    for by in (1, 2, 3):
        copy = send(gtot, ft.at[2, part(y)], h_s.at[by - 1], h_r.at[by - 1], dev(y=turn(y, by)))
        copy.start()
        started.append(copy)
    own_plane(1)
    other_plane(1)

    eye = jnp.where(
        lax.broadcasted_iota(jnp.int32, (BLK, BLK), 0) == lax.broadcasted_iota(jnp.int32, (BLK, BLK), 1), 1.0, 0.0
    )

    def put(slot, value, column):
        high = value.astype(BF16)
        low = (value - high.astype(F32)).astype(BF16)
        span = slice(column * BLK, (column + 1) * BLK)
        rhs[slot, 0:BLK, span] = high
        rhs[slot, BLK : 2 * BLK, span] = low
        rhs[slot, 2 * BLK :, span] = high
        if column == 0:
            lhs[slot, :, 0:BLK] = high
            lhs[slot, :, BLK : 2 * BLK] = high
            lhs[slot, :, 2 * BLK :] = low

    def dot(a, b):
        return jnp.dot(a, b, preferred_element_type=F32)

    def inverses(slots):
        scale = {}
        for s in slots:
            block = {rc: ft[s, n * 128 : (n + 1) * 128].astype(F32) for n, rc in enumerate(BLOCKS)}
            for r in range(3):
                for k in range(3):
                    tile = block[r, k] if r <= k else block[k, r].T
                    acc[s, r * 128 : (r + 1) * 128, k * 128 : (k + 1) * 128] = tile
        for s in slots:
            factor = acc[s] * (1.0 / 8192.0) + DAMPING * eye
            bound = jnp.max(jnp.sum(jnp.abs(factor), axis=1, keepdims=True), axis=0, keepdims=True)
            scale[s] = 1.0 / bound
            residue = eye - factor * scale[s]
            acc[s] = eye + residue
            put(s, residue, 0)
            put(s, acc[s], 1)
        for s in slots:
            put(s, dot(lhs[s], rhs[s, :, :BLK]), 0)
        for _ in range(2):
            for s in slots:
                both = dot(lhs[s], rhs[s])
                acc[s] += both[:, BLK:]
                put(s, both[:, :BLK], 0)
                put(s, acc[s], 1)
        for s in slots:
            acc[s] += dot(lhs[s], rhs[s, :, BLK:])
            square = dot(lhs[s, :, :BLK], rhs[s, :BLK, :BLK]).astype(BF16)
            acc[s] += dot(square, acc[s].astype(BF16))
        return [(acc[s] * scale[s]).astype(BF16) for s in slots]

    for by in (1, 2, 3):
        send(gtot, ft.at[2, part(y)], h_s.at[by - 1], h_r.at[by - 1], dev(y=turn(y, by))).wait_recv()
    ginv[c] = inverses((2,))[0]
    swap = send(ginv.at[c], ginv.at[c], i_s, i_r, dev(c=other))
    swap.start()
    load_w.wait()
    for layer in (0, 1):
        for yy in range(4):
            mine = (x == x_src) & (c == layer) & (y == yy)

            @pl.when(jnp.logical_not(mine))
            def _():
                send(
                    dtot.at[0, 0], ft.at[layer, part(yy)], e_s.at[0, 0, 0], e_r.at[layer, yy], dev(c=other)
                ).wait_recv()
    for layer, inverse in enumerate(inverses((0, 1))):
        left[layer] = dot(inverse, wv[layer]).astype(BF16)
    swap.wait()
    for layer in (0, 1):
        out[layer] = dot(left[layer], ginv[layer]).astype(BF16)

    for copy in started:
        copy.wait_send()
    for t in range(4):
        @pl.when(z != 2 * lax.rem(x, 2) + t // 2)
        def _():
            send(cs.at[0], crec.at[0, 0], c_s.at[t], c_r.at[0, 0], dev(c=other)).wait_send()

    @pl.when(active)
    def _():
        for e in (0, 1):
            cross(e).wait_send()
        for plane in (0, 1):
            for e in (0, 1):
                for by in range(4):
                    copy = send(dtot.at[0, 0], ft.at[0, part(0)], e_s.at[plane, e, by], e_r.at[0, 0], dev(c=other))
                    if by:
                        copy.wait_send()
                    else:
                        @pl.when((plane * 2 + x // 2 != y) | (c != e))
                        def _():
                            copy.wait_send()


def shards(hidden_acts, out_grads, token_picks, weight_grads):
    dma = pltpu.SemaphoreType.DMA
    vmem = pltpu.VMEM
    return pl.pallas_call(
        kernel,
        out_shape=jax.ShapeDtypeStruct(weight_grads.shape, BF16),
        in_specs=[
            pl.BlockSpec(memory_space=pl.ANY),
            pl.BlockSpec(memory_space=pl.ANY),
            pl.BlockSpec(memory_space=vmem),
            pl.BlockSpec(memory_space=pl.ANY),
        ],
        out_specs=pl.BlockSpec(memory_space=vmem),
        scratch_shapes=[
            vmem(hidden_acts.shape, BF16), vmem(out_grads.shape, BF16), vmem(weight_grads.shape, BF16),
            vmem((POOL, BLK), BF16),
            vmem((5, ROWS, 128), BF16), vmem((5, ROWS, 128), BF16), vmem((5, ROWS, 128), F32), vmem((5, ROWS, 128), BF16),
            vmem((3, 5, PART, 128), BF16), vmem((5, PART, 128), F32), vmem((5, PART, 128), BF16),
            vmem((3, 2, PART, 128), BF16), vmem((3, PART, 128), BF16), vmem((2, 2, PART, 128), BF16),
            vmem((PART, 128), BF16), vmem((3, ROWS, 128), BF16),
            vmem((3, BLK, 3 * BLK), BF16), vmem((3, 3 * BLK, 2 * BLK), BF16), vmem((3, BLK, BLK), F32),
            vmem((2, BLK, BLK), BF16), vmem((2, BLK, BLK), BF16),
            dma((11,)), dma((5,)), dma((5,)), dma((5, 3)), dma((5, 3)), dma((4,)), dma((3, 2)), dma((3,)), dma((3,)),
            dma((2,)), dma((2,)), dma((2, 2, 4)), dma((2, 4)), dma((3,)), dma((3,)), dma, dma,
        ],
        compiler_params=pltpu.CompilerParams(
            collective_id=0, has_side_effects=True, vmem_limit_bytes=58 * 2**20
        ),
    )(hidden_acts, out_grads, token_picks, weight_grads)


def solution(mesh):
    placed = (P(None, "dp", "mp"), P(None, "dp", "mp"), P("dp", None), P(None, "dp", "mp"))
    return jax.shard_map(shards, mesh=mesh, in_specs=placed, out_specs=P(None, "dp", "mp"), check_vma=False)
```

time: 60 us -> 53.1 us (0.89)
  the two profiles are of different devices: /device:TPU:28 before, /device:TPU:25 now
where the time goes in v2:
time: 53.1 us; the launch traced here: 53 us
  Pallas kernels  51 us (96%)
  local copies, waits for them, and re-layouts  1.94 us (4%)
    pallas_call x1, Pallas kernels, shards(): pl.pallas_call(kernel, out_shape=jax.ShapeDtypeStruct(weight_grads.shape,...  51 us
    unnamed x1, local copies, waits for them, and re-layouts  1.94 us

profile of v2, /device:TPU:25, one launch (start us, length us, event | category | flops | bytes accessed | tf_op | source)
XLA Modules:
  0.0 53.0 jit_solution(16115058096190418725)
XLA Ops:
  0.0 51.0 %shard_map.46 = bf16[2,384,384]{2,1,0:T(8,128)(2,1)} custom-call(bf16[2,512,1536]{2,1,0:T(8,128)(2,1)} %hid_hbm.1, bf16[2,512,384]{2,1,0:T(8,128)(2,1)} %grd_hbm.1, s32[1,512]{1,0:T(1,128)} %picks.1, bf16[2,384,384]{2,1,0:T(8,128)(2,1)} %w_hbm.1), custom_call_target="tpu_custom_call" | custom-call | tf_op jit(solution)/shard_map/pallas_call | solution.py:305
  51.1 1.9 %copy.6 = bf16[2,384,384]{2,1,0:T(8,128)(2,1)} copy(bf16[2,384,384]{2,1,0:T(8,128)(2,1)} %shard_map.46) | data formatting | bytes 1179648

commit v3 on v2

--- a/solution.py
+++ b/solution.py
@@ -8,14 +8,13 @@
 BLK = 384
 SAMPLE = 256
 POOL = 512
-ROWS = 768
-PART = 192
+ROWS = 640
+PART = 160
 DAMPING = 0.1
 MESH = pl.DeviceIdType.MESH
 F32 = jnp.float32
 BF16 = jnp.bfloat16
 ORDER = (0, 2, 4, 1, 3)
-BLOCKS = ((0, 0), (0, 1), (0, 2), (1, 1), (1, 2), (2, 2))
 
 
 def kernel(
@@ -27,7 +26,10 @@
     c, z, y = lax.rem(i, 2), lax.rem(i // 2, 4), i // 8
     zh, x = m // 4, lax.rem(m, 4)
     active = z // 2 == lax.rem(x, 2)
+    x_pair = x + 1 - 2 * lax.rem(x, 2)
     x_src = lax.rem(y, 2) * 2 + z // 2
+    x_from = jnp.where(zh == y // 2, x_src, x_src + 1 - 2 * lax.rem(x_src, 2))
+    y_goal = jnp.where(active, zh, 1 - zh) * 2 + x // 2
 
     def dev(y=y, z=z, c=c, zh=zh, x=x):
         return ((y * 4 + z) * 2 + c, zh * 4 + x)
@@ -43,28 +45,9 @@
     def part(q):
         return pl.ds(pl.multiple_of(q * PART, PART), PART)
 
-    barrier = pltpu.get_barrier_semaphore()
-
-    def greet(to):
-        pl.semaphore_signal(barrier, inc=1, device_id=to, device_id_type=MESH)
-
-    greet(dev(c=1 - c))
-    greet(dev(zh=1 - zh))
-    for by in (1, 2, 3):
-        greet(dev(y=turn(y, by)))
-        greet(dev(z=turn(z, by)))
-    for cc in (0, 1):
-        for by in range(4):
-            if by:
-                greet(dev(x=x_src, y=turn(y, by), c=cc))
-            else:
-                @pl.when((x_src != x) | (c != cc))
-                def _():
-                    greet(dev(x=x_src, c=cc))
-
     other = 1 - c
     loads = {}
-    for n, (own_layer, t) in enumerate([(own_layer, t) for own_layer in (0, 1) for t in ORDER]):
+    for n, (t, own_layer) in enumerate([(t, own_layer) for t in ORDER for own_layer in (0, 1)]):
         layer = c if own_layer else other
         if t == 4:
             copy = pltpu.make_async_copy(grd_hbm.at[layer], grd.at[layer], load_sem.at[n])
@@ -76,21 +59,53 @@
     load_w = pltpu.make_async_copy(w_hbm, wv, load_sem.at[10])
     load_w.start()
 
+    barrier = pltpu.get_barrier_semaphore()
+
+    def greet(to):
+        pl.semaphore_signal(barrier, inc=1, device_id=to, device_id_type=MESH)
+
+    greet(dev(c=1 - c))
+    greet(dev(zh=1 - zh, x=x_pair))
+    for by in (1, 2, 3):
+        greet(dev(y=turn(y, by)))
+        greet(dev(z=turn(z, by)))
+    for cc in (0, 1):
+        for by in range(4):
+            if by:
+                greet(dev(x=x_from, y=turn(y, by), c=cc))
+            else:
+                @pl.when((x_from != x) | (c != cc))
+                def _():
+                    greet(dev(x=x_from, c=cc))
+
     token = lax.broadcasted_iota(jnp.int32, (POOL, SAMPLE), 0)
     hit = jnp.where(token == picks[:, :SAMPLE], 1.0, 0.0)
     mask[...] = jnp.broadcast_to(jnp.max(hit, axis=1, keepdims=True), (POOL, BLK)).astype(BF16)
 
+    row = lax.broadcasted_iota(jnp.int32, (128, 128), 0)
+    col = lax.broadcasted_iota(jnp.int32, (128, 128), 1)
+
+    def diagonal(block):
+        return jnp.sum(jnp.where(row == col, block, 0.0), axis=0, keepdims=True)
+
     def gram(tile, dst):
         masked = tile * mask[...]
-        row = 0
-        for r in range(3):
-            g = lax.dot_general(
+        g0, g1, g2 = [
+            lax.dot_general(
                 masked[:, r * 128 : (r + 1) * 128], tile[:, r * 128 :], (((0,), (0,)), ((), ())),
                 preferred_element_type=F32,
             )
-            for k in range(3 - r):
-                dst[row : row + 128, :] = g[:, k * 128 : (k + 1) * 128].astype(dst.dtype)
-                row += 128
+            for r in range(3)
+        ]
+        g11 = g1[:, :128]
+        folded = jnp.where((row > col)[:64] & (col < 64)[:64], pltpu.roll(g2[64:], 64, 1), g2[:64])
+        lines = jnp.where(row[:64] == 0, diagonal(g11), jnp.where(row[:64] == 1, diagonal(g2), 0.0))
+        dst[0:128, :] = jnp.where(row <= col, g0[:, :128], g11).astype(dst.dtype)
+        dst[128:256, :] = g0[:, 128:256].astype(dst.dtype)
+        dst[256:384, :] = g0[:, 256:].astype(dst.dtype)
+        dst[384:512, :] = g1[:, 128:].astype(dst.dtype)
+        dst[512:576, :] = folded.astype(dst.dtype)
+        dst[576:640, :] = lines.astype(dst.dtype)
 
     def gram_of(own_layer, t, dst):
         loads[own_layer, t].wait()
@@ -98,18 +113,14 @@
         gram(grd[layer] if t == 4 else hid[layer, :, t * BLK : (t + 1) * BLK], dst.at[t])
 
     started, from_sibling, from_y, from_z = [], {}, {}, {}
-    for n, t in enumerate(ORDER):
-        gram_of(0, t, abuf)
-        if n == 0:
-            pl.semaphore_wait(barrier, 8 + jnp.where(active, jnp.where(lax.rem(y, 2) == x // 2, 15, 16), 0))
+
+    def to_sibling(t):
         copy = send(abuf.at[t], arec.at[t], a_s.at[t], a_r.at[t], dev(c=other))
         copy.start()
         started.append(copy)
         from_sibling[t] = copy
-    for t in ORDER:
-        gram_of(1, t, own)
-
-    for t in ORDER:
+
+    def to_quarters(t):
         from_sibling[t].wait_recv()
         total = own[t] + arec[t].astype(F32)
         own[t] = total
@@ -121,6 +132,16 @@
             started.append(copy)
             from_y[t, by] = copy
 
+    for n, t in enumerate(ORDER):
+        gram_of(0, t, abuf)
+        if n == 0:
+            pl.semaphore_wait(barrier, jnp.where(y == y_goal, 15, 16))
+        to_sibling(t)
+        gram_of(1, t, own)
+        if n:
+            to_quarters(ORDER[n - 1])
+    to_quarters(ORDER[-1])
+
     def sum_y(t):
         for by in (1, 2, 3):
             from_y[t, by].wait_recv()
@@ -139,12 +160,10 @@
             slot = lax.rem(z - goal + 4, 4) - 1
             send(cs.at[t], crec.at[slot, t % 2], c_s.at[t], c_r.at[slot, t % 2], dev(z=goal)).start()
 
-    def spread(plane, e):
-        y_goal = plane * 2 + x // 2
+    def spread(e):
         for by in (2, 1, 3, 0):
             copy = send(
-                dtot.at[plane, e], ft.at[c, part(y)], e_s.at[plane, e, by], e_r.at[c, y],
-                dev(y=y_goal, c=e, x=turn(x, by)),
+                dtot.at[e], ft.at[c, part(y)], e_s.at[e, by], e_r.at[c, y], dev(y=y_goal, c=e, x=turn(x, by))
             )
             if by:
                 copy.start()
@@ -153,16 +172,16 @@
 
                 @pl.when(here)
                 def _():
-                    ft[c, part(y)] = dtot[plane, e]
+                    ft[c, part(y)] = dtot[e]
 
                 @pl.when(jnp.logical_not(here))
                 def _():
                     copy.start()
 
     def cross(e):
-        return send(dtot.at[zh, e], dtot.at[zh, e], d_s.at[e], d_r.at[e], dev(zh=1 - zh))
-
-    def own_plane(e):
+        return send(dtot.at[e], dtot.at[e], d_s.at[e], d_r.at[e], dev(zh=1 - zh, x=x_pair))
+
+    def from_users(e):
         @pl.when(active)
         def _():
             for by in (1, 2, 3):
@@ -170,41 +189,47 @@
             total = ysum[2 * lax.rem(z, 2) + e]
             for by in (1, 2, 3):
                 total += crec[by - 1, e].astype(F32)
-            dtot[zh, e] = total.astype(BF16)
+            dtot[e] = total.astype(BF16)
             cross(e).start()
-            spread(zh, e)
-
-    def other_plane(e):
-        @pl.when(active)
+            spread(e)
+
+    def from_cross(e):
+        @pl.when(jnp.logical_not(active))
         def _():
-            send(dtot.at[zh, e], dtot.at[1 - zh, e], d_s.at[e], d_r.at[e], dev(zh=1 - zh)).wait_recv()
-            spread(1 - zh, e)
+            cross(e).wait_recv()
+            spread(e)
+
+    def to_every_z():
+        sum_y(4)
+        for by in (1, 2, 3):
+            copy = send(cs.at[4], grec.at[by - 1], g_s.at[by - 1], g_r.at[by - 1], dev(z=turn(z, by)))
+            copy.start()
+            started.append(copy)
+            from_z[by] = copy
+
+    def gather_gradient_tile():
+        for by in (1, 2, 3):
+            from_z[by].wait_recv()
+        total = ysum[4]
+        for by in (1, 2, 3):
+            total += grec[by - 1].astype(F32)
+        gtot[...] = total.astype(BF16)
+        ft[2, part(y)] = gtot[...]
+        for by in (1, 2, 3):
+            copy = send(gtot, ft.at[2, part(y)], h_s.at[by - 1], h_r.at[by - 1], dev(y=turn(y, by)))
+            copy.start()
+            started.append(copy)
 
     to_users(0)
     to_users(2)
-    sum_y(4)
-    for by in (1, 2, 3):
-        copy = send(cs.at[4], grec.at[by - 1], g_s.at[by - 1], g_r.at[by - 1], dev(z=turn(z, by)))
-        copy.start()
-        started.append(copy)
-        from_z[by] = copy
-    own_plane(0)
+    to_every_z()
+    from_users(0)
     to_users(1)
     to_users(3)
-    other_plane(0)
-    for by in (1, 2, 3):
-        from_z[by].wait_recv()
-    total = ysum[4]
-    for by in (1, 2, 3):
-        total += grec[by - 1].astype(F32)
-    gtot[...] = total.astype(BF16)
-    ft[2, part(y)] = gtot[...]
-    for by in (1, 2, 3):
-        copy = send(gtot, ft.at[2, part(y)], h_s.at[by - 1], h_r.at[by - 1], dev(y=turn(y, by)))
-        copy.start()
-        started.append(copy)
-    own_plane(1)
-    other_plane(1)
+    from_cross(0)
+    gather_gradient_tile()
+    from_users(1)
+    from_cross(1)
 
     eye = jnp.where(
         lax.broadcasted_iota(jnp.int32, (BLK, BLK), 0) == lax.broadcasted_iota(jnp.int32, (BLK, BLK), 1), 1.0, 0.0
@@ -228,7 +253,22 @@
     def inverses(slots):
         scale = {}
         for s in slots:
-            block = {rc: ft[s, n * 128 : (n + 1) * 128].astype(F32) for n, rc in enumerate(BLOCKS)}
+            def rows(first, count):
+                return ft[s, first : first + count].astype(F32)
+
+            mixed, turned = rows(0, 128), rows(0, 128).T
+            folded = rows(512, 64)
+            lines = rows(576, 16)
+            square = jnp.concatenate([folded, pltpu.roll(folded, 64, 1)], axis=0)
+            upright = ((row < 64) & (row <= col)) | ((row >= 64) & (col >= 64) & (row > col))
+            block = {
+                (0, 0): jnp.where(row <= col, mixed, turned),
+                (0, 1): rows(128, 128),
+                (0, 2): rows(256, 128),
+                (1, 1): jnp.where(row == col, lines[0:1], jnp.where(row > col, mixed, turned)),
+                (1, 2): rows(384, 128),
+                (2, 2): jnp.where((row == col) & (row >= 64), lines[1:2], jnp.where(upright, square, square.T)),
+            }
             for r in range(3):
                 for k in range(3):
                     tile = block[r, k] if r <= k else block[k, r].T
@@ -263,12 +303,12 @@
     load_w.wait()
     for layer in (0, 1):
         for yy in range(4):
-            mine = (x == x_src) & (c == layer) & (y == yy)
+            mine = (x == x_from) & (c == layer) & (y == yy)
 
             @pl.when(jnp.logical_not(mine))
             def _():
                 send(
-                    dtot.at[0, 0], ft.at[layer, part(yy)], e_s.at[0, 0, 0], e_r.at[layer, yy], dev(c=other)
+                    dtot.at[0], ft.at[layer, part(yy)], e_s.at[0, 0], e_r.at[layer, yy], dev(c=other)
                 ).wait_recv()
     for layer, inverse in enumerate(inverses((0, 1))):
         left[layer] = dot(inverse, wv[layer]).astype(BF16)
@@ -287,16 +327,16 @@
     def _():
         for e in (0, 1):
             cross(e).wait_send()
-        for plane in (0, 1):
-            for e in (0, 1):
-                for by in range(4):
-                    copy = send(dtot.at[0, 0], ft.at[0, part(0)], e_s.at[plane, e, by], e_r.at[0, 0], dev(c=other))
-                    if by:
-                        copy.wait_send()
-                    else:
-                        @pl.when((plane * 2 + x // 2 != y) | (c != e))
-                        def _():
-                            copy.wait_send()
+
+    for e in (0, 1):
+        for by in range(4):
+            copy = send(dtot.at[0], ft.at[0, part(0)], e_s.at[e, by], e_r.at[0, 0], dev(c=other))
+            if by:
+                copy.wait_send()
+            else:
+                @pl.when((y_goal != y) | (c != e))
+                def _():
+                    copy.wait_send()
 
 
 def shards(hidden_acts, out_grads, token_picks, weight_grads):
@@ -317,15 +357,15 @@
             vmem((POOL, BLK), BF16),
             vmem((5, ROWS, 128), BF16), vmem((5, ROWS, 128), BF16), vmem((5, ROWS, 128), F32), vmem((5, ROWS, 128), BF16),
             vmem((3, 5, PART, 128), BF16), vmem((5, PART, 128), F32), vmem((5, PART, 128), BF16),
-            vmem((3, 2, PART, 128), BF16), vmem((3, PART, 128), BF16), vmem((2, 2, PART, 128), BF16),
+            vmem((3, 2, PART, 128), BF16), vmem((3, PART, 128), BF16), vmem((2, PART, 128), BF16),
             vmem((PART, 128), BF16), vmem((3, ROWS, 128), BF16),
             vmem((3, BLK, 3 * BLK), BF16), vmem((3, 3 * BLK, 2 * BLK), BF16), vmem((3, BLK, BLK), F32),
             vmem((2, BLK, BLK), BF16), vmem((2, BLK, BLK), BF16),
             dma((11,)), dma((5,)), dma((5,)), dma((5, 3)), dma((5, 3)), dma((4,)), dma((3, 2)), dma((3,)), dma((3,)),
-            dma((2,)), dma((2,)), dma((2, 2, 4)), dma((2, 4)), dma((3,)), dma((3,)), dma, dma,
+            dma((2,)), dma((2,)), dma((2, 4)), dma((2, 4)), dma((3,)), dma((3,)), dma, dma,
         ],
         compiler_params=pltpu.CompilerParams(
-            collective_id=0, has_side_effects=True, vmem_limit_bytes=58 * 2**20
+            collective_id=0, has_side_effects=True, vmem_limit_bytes=53 * 2**20
         ),
     )(hidden_acts, out_grads, token_picks, weight_grads)
 

time: 53.1 us -> 47.6 us (0.90)
  the two profiles are of different devices: /device:TPU:25 before, /device:TPU:2 now
where the time goes in v3:
time: 47.6 us
  Pallas kernels  46 us (97%)
  local copies, waits for them, and re-layouts  1.5 us (3%)
    pallas_call x1, Pallas kernels, shards(): pl.pallas_call(kernel, out_shape=jax.ShapeDtypeStruct(weight_grads.shape,...  46 us
    unnamed x3, local copies, waits for them, and re-layouts  1.5 us

profile of v3, /device:TPU:2, one launch (start us, length us, event | category | flops | bytes accessed | tf_op | source)
XLA Modules:
  0.0 47.6 jit_solution(927268214540865404)
XLA Ops:
  0.0 0.0 copy-start
  0.0 0.7 %copy-done = s32[1,512]{1,0:T(1,128)S(1)} copy-done((s32[1,512]{1,0:T(1,128)S(1)}, s32[1,512]{1,0:T(1,128)}, u32[]{:S(2)}) %copy-start) | copy-done | bytes 2072
  0.7 46.0 %shard_map.46 = bf16[2,384,384]{2,1,0:T(8,128)(2,1)S(1)} custom-call(bf16[2,512,1536]{2,1,0:T(8,128)(2,1)} %hid_hbm.1, bf16[2,512,384]{2,1,0:T(8,128)(2,1)} %grd_hbm.1, s32[1,512]{1,0:T(1,128)S(1)} %copy-done, bf16[2,384,384]{2,1,0:T(8,128)(2,1)} %w_hbm.1), custom_call_target="tpu_custom_call" | custom-call | tf_op jit(solution)/shard_map/pallas_call | solution.py:345
  46.7 0.8 %copy.6 = bf16[2,384,384]{2,1,0:T(8,128)(2,1)} copy(bf16[2,384,384]{2,1,0:T(8,128)(2,1)S(1)} %shard_map.46) | data formatting | bytes 1179648
Async XLA Ops:
  0.0 0.7 %copy-start = (s32[1,512]{1,0:T(1,128)S(1)}, s32[1,512]{1,0:T(1,128)}, u32[]{:S(2)}) copy-start(s32[1,512]{1,0:T(1,128)} %picks.1) | copy-start | bytes 6148

commit v4 on v3

--- a/solution.py
+++ b/solution.py
@@ -10,6 +10,7 @@
 POOL = 512
 ROWS = 640
 PART = 160
+SLICE = 48
 DAMPING = 0.1
 MESH = pl.DeviceIdType.MESH
 F32 = jnp.float32
@@ -19,8 +20,8 @@
 
 def kernel(
     hid_hbm, grd_hbm, picks, w_hbm, out,
-    hid, grd, wv, mask, abuf, arec, own, s1, brec, ysum, cs, crec, grec, dtot, gtot, ft, lhs, rhs, acc, ginv, left,
-    load_sem, a_s, a_r, b_s, b_r, c_s, c_r, g_s, g_r, d_s, d_r, e_s, e_r, h_s, h_r, i_s, i_r,
+    hid, grd, wv, mask, abuf, arec, own, s1, brec, ysum, cs, crec, grec, dtot, gtot, gsum, gpart, gz, ft, lhs, rhs, acc, ginv, left,
+    load_sem, a_s, a_r, b_s, b_r, c_s, c_r, g_s, g_r, k_s, k_r, d_s, d_r, e_s, e_r, h_s, h_r, i_s, i_r,
 ):
     i, m = lax.axis_index("dp"), lax.axis_index("mp")
     c, z, y = lax.rem(i, 2), lax.rem(i // 2, 4), i // 8
@@ -160,6 +161,44 @@
             slot = lax.rem(z - goal + 4, 4) - 1
             send(cs.at[t], crec.at[slot, t % 2], c_s.at[t], c_r.at[slot, t % 2], dev(z=goal)).start()
 
+    def rows_of(q):
+        return pl.ds(pl.multiple_of(q * SLICE, SLICE), SLICE)
+
+    def to_slices():
+        sum_y(4)
+        gsum[0:PART] = ysum[4]
+        gpart[0:PART] = cs[4]
+        gsum[PART:] = jnp.zeros((4 * SLICE - PART, 128), F32)
+        gpart[PART:] = jnp.zeros((4 * SLICE - PART, 128), BF16)
+        for by in (1, 2, 3):
+            to = turn(z, by)
+            copy = send(gpart.at[rows_of(to)], grec.at[by - 1], g_s.at[by - 1], g_r.at[by - 1], dev(z=to))
+            copy.start()
+            started.append(copy)
+            from_z[by] = copy
+
+    def gather_slices():
+        for by in (1, 2, 3):
+            from_z[by].wait_recv()
+        total = gsum[rows_of(z)]
+        for by in (1, 2, 3):
+            total += grec[by - 1].astype(F32)
+        gtot[...] = total.astype(BF16)
+        gz[rows_of(z)] = gtot[...]
+        for by in (1, 2, 3):
+            copy = send(gtot, gz.at[rows_of(z)], k_s.at[by - 1], k_r.at[by - 1], dev(z=turn(z, by)))
+            copy.start()
+            started.append(copy)
+
+    def gather_gradient_tile():
+        for by in (1, 2, 3):
+            send(gtot, gz.at[rows_of(z)], k_s.at[by - 1], k_r.at[by - 1], dev(z=turn(z, by))).wait_recv()
+        ft[2, part(y)] = gz[0:PART]
+        for by in (1, 2, 3):
+            copy = send(gz.at[0:PART], ft.at[2, part(y)], h_s.at[by - 1], h_r.at[by - 1], dev(y=turn(y, by)))
+            copy.start()
+            started.append(copy)
+
     def spread(e):
         for by in (2, 1, 3, 0):
             copy = send(
@@ -199,32 +238,12 @@
             cross(e).wait_recv()
             spread(e)
 
-    def to_every_z():
-        sum_y(4)
-        for by in (1, 2, 3):
-            copy = send(cs.at[4], grec.at[by - 1], g_s.at[by - 1], g_r.at[by - 1], dev(z=turn(z, by)))
-            copy.start()
-            started.append(copy)
-            from_z[by] = copy
-
-    def gather_gradient_tile():
-        for by in (1, 2, 3):
-            from_z[by].wait_recv()
-        total = ysum[4]
-        for by in (1, 2, 3):
-            total += grec[by - 1].astype(F32)
-        gtot[...] = total.astype(BF16)
-        ft[2, part(y)] = gtot[...]
-        for by in (1, 2, 3):
-            copy = send(gtot, ft.at[2, part(y)], h_s.at[by - 1], h_r.at[by - 1], dev(y=turn(y, by)))
-            copy.start()
-            started.append(copy)
-
     to_users(0)
     to_users(2)
-    to_every_z()
+    to_slices()
     from_users(0)
     to_users(1)
+    gather_slices()
     to_users(3)
     from_cross(0)
     gather_gradient_tile()
@@ -240,12 +259,12 @@
         low = (value - high.astype(F32)).astype(BF16)
         span = slice(column * BLK, (column + 1) * BLK)
         rhs[slot, 0:BLK, span] = high
-        rhs[slot, BLK : 2 * BLK, span] = low
-        rhs[slot, 2 * BLK :, span] = high
+        rhs[slot, BLK : 2 * BLK, span] = high
+        rhs[slot, 2 * BLK :, span] = low
         if column == 0:
             lhs[slot, :, 0:BLK] = high
-            lhs[slot, :, BLK : 2 * BLK] = high
-            lhs[slot, :, 2 * BLK :] = low
+            lhs[slot, :, BLK : 2 * BLK] = low
+            lhs[slot, :, 2 * BLK :] = high
 
     def dot(a, b):
         return jnp.dot(a, b, preferred_element_type=F32)
@@ -290,13 +309,13 @@
                 put(s, both[:, :BLK], 0)
                 put(s, acc[s], 1)
         for s in slots:
-            acc[s] += dot(lhs[s], rhs[s, :, BLK:])
+            acc[s] += dot(lhs[s, :, : 2 * BLK], rhs[s, : 2 * BLK, BLK:])
             square = dot(lhs[s, :, :BLK], rhs[s, :BLK, :BLK]).astype(BF16)
             acc[s] += dot(square, acc[s].astype(BF16))
         return [(acc[s] * scale[s]).astype(BF16) for s in slots]
 
     for by in (1, 2, 3):
-        send(gtot, ft.at[2, part(y)], h_s.at[by - 1], h_r.at[by - 1], dev(y=turn(y, by))).wait_recv()
+        send(gz.at[0:PART], ft.at[2, part(y)], h_s.at[by - 1], h_r.at[by - 1], dev(y=turn(y, by))).wait_recv()
     ginv[c] = inverses((2,))[0]
     swap = send(ginv.at[c], ginv.at[c], i_s, i_r, dev(c=other))
     swap.start()
@@ -357,11 +376,12 @@
             vmem((POOL, BLK), BF16),
             vmem((5, ROWS, 128), BF16), vmem((5, ROWS, 128), BF16), vmem((5, ROWS, 128), F32), vmem((5, ROWS, 128), BF16),
             vmem((3, 5, PART, 128), BF16), vmem((5, PART, 128), F32), vmem((5, PART, 128), BF16),
-            vmem((3, 2, PART, 128), BF16), vmem((3, PART, 128), BF16), vmem((2, PART, 128), BF16),
-            vmem((PART, 128), BF16), vmem((3, ROWS, 128), BF16),
+            vmem((3, 2, PART, 128), BF16), vmem((3, SLICE, 128), BF16), vmem((2, PART, 128), BF16),
+            vmem((SLICE, 128), BF16), vmem((4 * SLICE, 128), F32), vmem((4 * SLICE, 128), BF16), vmem((4 * SLICE, 128), BF16),
+            vmem((3, ROWS, 128), BF16),
             vmem((3, BLK, 3 * BLK), BF16), vmem((3, 3 * BLK, 2 * BLK), BF16), vmem((3, BLK, BLK), F32),
             vmem((2, BLK, BLK), BF16), vmem((2, BLK, BLK), BF16),
-            dma((11,)), dma((5,)), dma((5,)), dma((5, 3)), dma((5, 3)), dma((4,)), dma((3, 2)), dma((3,)), dma((3,)),
+            dma((11,)), dma((5,)), dma((5,)), dma((5, 3)), dma((5, 3)), dma((4,)), dma((3, 2)), dma((3,)), dma((3,)), dma((3,)), dma((3,)),
             dma((2,)), dma((2,)), dma((2, 4)), dma((2, 4)), dma((3,)), dma((3,)), dma, dma,
         ],
         compiler_params=pltpu.CompilerParams(

time: 47.6 us -> 46.4 us (0.975)
  Pallas kernels: 46 us -> 44.5 us
    pallas_call x1, Pallas kernels: 46 us -> 44.5 us  [shards(): pl.pallas_call(kernel, out_shape=jax.ShapeDtypeStruct(weight_grads.shape,...]
where the time goes in v4:
time: 46.4 us; the launch traced here: 46 us
  Pallas kernels  44.5 us (96%)
  local copies, waits for them, and re-layouts  1.5 us (3%)
    pallas_call x1, Pallas kernels, shards(): pl.pallas_call(kernel, out_shape=jax.ShapeDtypeStruct(weight_grads.shape,...  44.5 us
    unnamed x3, local copies, waits for them, and re-layouts  1.5 us

profile of v4, /device:TPU:2, one launch (start us, length us, event | category | flops | bytes accessed | tf_op | source)
XLA Modules:
  0.0 46.0 jit_solution(4033756615361294867)
XLA Ops:
  0.0 0.0 copy-start
  0.0 0.7 %copy-done = s32[1,512]{1,0:T(1,128)S(1)} copy-done((s32[1,512]{1,0:T(1,128)S(1)}, s32[1,512]{1,0:T(1,128)}, u32[]{:S(2)}) %copy-start) | copy-done | bytes 2072
  0.7 44.5 %shard_map.46 = bf16[2,384,384]{2,1,0:T(8,128)(2,1)S(1)} custom-call(bf16[2,512,1536]{2,1,0:T(8,128)(2,1)} %hid_hbm.1, bf16[2,512,384]{2,1,0:T(8,128)(2,1)} %grd_hbm.1, s32[1,512]{1,0:T(1,128)S(1)} %copy-done, bf16[2,384,384]{2,1,0:T(8,128)(2,1)} %w_hbm.1), custom_call_target="tpu_custom_call" | custom-call | tf_op jit(solution)/shard_map/pallas_call | solution.py:364
  45.2 0.8 %copy.6 = bf16[2,384,384]{2,1,0:T(8,128)(2,1)} copy(bf16[2,384,384]{2,1,0:T(8,128)(2,1)S(1)} %shard_map.46) | data formatting | bytes 1179648
Async XLA Ops:
  0.0 0.7 %copy-start = (s32[1,512]{1,0:T(1,128)S(1)}, s32[1,512]{1,0:T(1,128)}, u32[]{:S(2)}) copy-start(s32[1,512]{1,0:T(1,128)} %picks.1) | copy-start | bytes 6148

commit v5 on v4

--- a/solution.py
+++ b/solution.py
@@ -55,21 +55,16 @@
         else:
             span = pl.ds(t * BLK, BLK)
             copy = pltpu.make_async_copy(hid_hbm.at[layer, :, span], hid.at[layer, :, span], load_sem.at[n])
-        copy.start()
         loads[own_layer, t] = copy
-    load_w = pltpu.make_async_copy(w_hbm, wv, load_sem.at[10])
-    load_w.start()
+        if n < 2:
+            copy.start()
 
     barrier = pltpu.get_barrier_semaphore()
 
     def greet(to):
         pl.semaphore_signal(barrier, inc=1, device_id=to, device_id_type=MESH)
 
-    greet(dev(c=1 - c))
     greet(dev(zh=1 - zh, x=x_pair))
-    for by in (1, 2, 3):
-        greet(dev(y=turn(y, by)))
-        greet(dev(z=turn(z, by)))
     for cc in (0, 1):
         for by in range(4):
             if by:
@@ -78,6 +73,16 @@
                 @pl.when((x_from != x) | (c != cc))
                 def _():
                     greet(dev(x=x_from, c=cc))
+
+    for by in (1, 2, 3):
+        greet(dev(y=turn(y, by)))
+        greet(dev(z=turn(z, by)))
+    greet(dev(c=1 - c))
+
+    for copy in list(loads.values())[2:]:
+        copy.start()
+    load_w = pltpu.make_async_copy(w_hbm, wv, load_sem.at[10])
+    load_w.start()
 
     token = lax.broadcasted_iota(jnp.int32, (POOL, SAMPLE), 0)
     hit = jnp.where(token == picks[:, :SAMPLE], 1.0, 0.0)
@@ -134,14 +139,15 @@
             from_y[t, by] = copy
 
     for n, t in enumerate(ORDER):
-        gram_of(0, t, abuf)
         if n == 0:
+            gram_of(0, t, abuf)
             pl.semaphore_wait(barrier, jnp.where(y == y_goal, 15, 16))
-        to_sibling(t)
+            to_sibling(t)
+        if n + 1 < len(ORDER):
+            gram_of(0, ORDER[n + 1], abuf)
+            to_sibling(ORDER[n + 1])
         gram_of(1, t, own)
-        if n:
-            to_quarters(ORDER[n - 1])
-    to_quarters(ORDER[-1])
+        to_quarters(t)
 
     def sum_y(t):
         for by in (1, 2, 3):

time: 46.4 us -> 46.1 us (level)
  no operation moved by 1% of the time
where the time goes in v5:
time: 46.1 us; the launch traced here: 46 us
  Pallas kernels  44.5 us (97%)
  local copies, waits for them, and re-layouts  1.5 us (3%)
    pallas_call x1, Pallas kernels, shards(): pl.pallas_call(kernel, out_shape=jax.ShapeDtypeStruct(weight_grads.shape,...  44.5 us
    unnamed x3, local copies, waits for them, and re-layouts  1.5 us

profile of v5, /device:TPU:2, one launch (start us, length us, event | category | flops | bytes accessed | tf_op | source)
XLA Modules:
  0.0 46.0 jit_solution(5550584934587416532)
XLA Ops:
  0.0 0.0 copy-start
  0.0 0.7 %copy-done = s32[1,512]{1,0:T(1,128)S(1)} copy-done((s32[1,512]{1,0:T(1,128)S(1)}, s32[1,512]{1,0:T(1,128)}, u32[]{:S(2)}) %copy-start) | copy-done | bytes 2072
  0.7 44.5 %shard_map.46 = bf16[2,384,384]{2,1,0:T(8,128)(2,1)S(1)} custom-call(bf16[2,512,1536]{2,1,0:T(8,128)(2,1)} %hid_hbm.1, bf16[2,512,384]{2,1,0:T(8,128)(2,1)} %grd_hbm.1, s32[1,512]{1,0:T(1,128)S(1)} %copy-done, bf16[2,384,384]{2,1,0:T(8,128)(2,1)} %w_hbm.1), custom_call_target="tpu_custom_call" | custom-call | tf_op jit(solution)/shard_map/pallas_call | solution.py:370
  45.2 0.8 %copy.6 = bf16[2,384,384]{2,1,0:T(8,128)(2,1)} copy(bf16[2,384,384]{2,1,0:T(8,128)(2,1)S(1)} %shard_map.46) | data formatting | bytes 1179648
Async XLA Ops:
  0.0 0.7 %copy-start = (s32[1,512]{1,0:T(1,128)S(1)}, s32[1,512]{1,0:T(1,128)}, u32[]{:S(2)}) copy-start(s32[1,512]{1,0:T(1,128)} %picks.1) | copy-start | bytes 6148
